TPU v7x, 512 devices: a whole 4x8x8 slice. The times are simulated.
512 devices in a mesh: region: 16 (over z_hi, y), worker: 32 (over z_lo, x, core).
Axes of the slice: x: 4, y: 8, z: 8 (z_hi: 2, z_lo: 4; z = z_hi * 4 + z_lo), core: 2. Of those that a mesh axis runs over, the one named last changes fastest.
Arguments:
- worker_start: bfloat16 [16, 128, 4096], P('region'), may hold values from -0.5 to 0.5
- inputs: bfloat16 [16, 32, 4, 256, 128], P('region', 'worker'), may hold values from -6 to 6
- teacher: bfloat16 [128, 4096], replicated, may hold values from -0.5 to 0.5
- regional_momentum: float32 [16, 128, 4096], P('region', 'worker'), may hold values from -1.5 to 1.5
- global_params: float32 [128, 4096], P('worker', 'region'), may hold values from -6 to 6
- global_momentum: float32 [128, 4096], P('worker', 'region'), may hold values from -1.5 to 1.5
- staleness: int32 [16], replicated, may hold values from 0 to 4
- arrival_order: int32 [16], replicated, may hold values from 0 to 15, as said below
- pull_slot: int32 [16], replicated, may hold values from 0 to 15, as said below
Outputs:
- momentum_regional: float32 [16, 128, 4096], P('region', 'worker')
- params_global: float32 [128, 4096], P('worker', 'region')
- momentum_global: float32 [128, 4096], P('worker', 'region')
- worker_params: float32 [16, 128, 4096], P('region')
Inputs may be any that keep to these rules, and one draw needn't show every extreme that they name: arrival_order is a permutation of the regions 0 .. 15. pull_slot[r] is at least the position of region r in arrival_order; the region that arrives first has slot 0.
All inputs are finite; a program needn't handle non-finite values.
Results may differ from a plain program's by a relative error of at most 0.00043.
Values sent between devices are 32-bit elements; how exact they have to be, the bound alone decides.
A program may use at most 64 MiB of HBM per device.

v0:
```python
import jax
import jax.numpy as jnp
from jax import lax
from jax.sharding import PartitionSpec as P

LOCAL_RATE = 0.3
REGION_BETA = 0.9
REGION_RATE = 1.0
GLOBAL_MU = 0.9
GLOBAL_RATE = 0.7


def residual_of(weights, micro_batch, teacher):
    target = jax.nn.silu(jnp.dot(micro_batch, teacher, preferred_element_type=jnp.float32))
    predicted = jnp.dot(
        micro_batch, weights.astype(jnp.bfloat16), preferred_element_type=jnp.float32
    )
    return (predicted - target).astype(jnp.bfloat16)


def gradient_of(micro_batch, residual):
    return lax.dot_general(
        micro_batch, residual, (((0,), (0,)), ((), ())), preferred_element_type=jnp.float32
    )


def merge_arrivals(deltas, region_dim, params_now, momentum_now, weights, arrival_order):

    def advance(state_pair, arrival):
        params_cur, momentum_cur = state_pair
        source = arrival_order[arrival]
        update = weights[source] * lax.dynamic_index_in_dim(
            deltas, source, region_dim, keepdims=False
        )
        momentum_cur = GLOBAL_MU * momentum_cur + update
        params_cur = params_cur - GLOBAL_RATE * (update + GLOBAL_MU * momentum_cur)
        return ((params_cur, momentum_cur), params_cur)

    return lax.scan(
        advance, (params_now, momentum_now), jnp.arange(arrival_order.shape[0], dtype=jnp.int32)
    )


def local(
    worker_start,
    inputs,
    teacher,
    regional_momentum,
    global_params,
    global_momentum,
    staleness,
    arrival_order,
    pull_slot,
):
    initial = worker_start[0]
    hidden = inputs[0, 0]
    shard_rows = regional_momentum.shape[1]
    step_scale = LOCAL_RATE / hidden.shape[1]
    start_weights = initial.astype(jnp.float32)
    local_steps = hidden.shape[0]
    current = start_weights
    for local_step in range(local_steps):
        residual = residual_of(current, hidden[local_step], teacher)
        current = current - step_scale * gradient_of(hidden[local_step], residual)
    pseudo = start_weights - current
    summed = lax.psum_scatter(pseudo, "worker", scatter_dimension=0, tiled=True)
    momentum_new = REGION_BETA * regional_momentum[0] + summed / lax.axis_size("worker")
    regional_delta = REGION_RATE * momentum_new
    weights = 1.0 / (1.0 + staleness.astype(jnp.float32))
    received = lax.all_to_all(
        regional_delta.reshape(shard_rows, 1, -1), "region", split_axis=2, concat_axis=1, tiled=True
    )
    (params_out, momentum_out), versions = merge_arrivals(
        received, 1, global_params, global_momentum, weights, arrival_order
    )
    select = (
        pull_slot[:, None] == jnp.arange(arrival_order.shape[0], dtype=jnp.int32)[None, :]
    ).astype(jnp.float32)
    pulled = jnp.einsum("dk,kic->idc", select, versions, precision=lax.Precision.HIGHEST)
    returned = lax.all_to_all(pulled, "region", split_axis=1, concat_axis=2, tiled=True)
    pulled_rows = returned.reshape(shard_rows, -1)
    worker_params = lax.all_gather(pulled_rows, "worker", axis=0, tiled=True)
    return (momentum_new[None], params_out, momentum_out, worker_params[None])


def solution(mesh):
    placed = (
        P("region", None, None),
        P("region", "worker", None, None, None),
        P(),
        P("region", "worker", None),
        P("worker", "region"),
        P("worker", "region"),
        P(),
        P(),
        P(),
    )
    return jax.shard_map(
        local,
        mesh=mesh,
        in_specs=placed,
        out_specs=(
            P("region", "worker", None),
            P("worker", "region"),
            P("worker", "region"),
            P("region", None, None),
        ),
        check_vma=False,
    )
```

profile of v0, /device:TPU:1, one launch (start us, length us, event | category | flops | bytes accessed | tf_op | source)
XLA Modules:
  0.0 580.1 jit_solution(9943884774316577426)
XLA Ops:
  7.2 1.2 copy-done
  8.4 3.5 fusion.39
  11.9 2.7 fusion.35
  14.6 2.6 fusion.31
  17.2 2.6 fusion.27
  19.9 0.7 copy.19
  20.5 5.6 fusion.17
  26.1 6.8 %fusion.15 = f32[128,4096]{0,1:T(8,128)} fusion(f32[128,4096]{0,1:T(8,128)} %fusion.17, f32[256,4096]{1,0:T(8,128)} %fusion.35, bf16[1,1,4,256,128]{4,3,2,1,0:T(8,128)(2,1)S(1)} %copy-done.4), kind=kOutput, calls=%fused_computation.25 | convolution fusion | flops 544735232 | bytes 10616832 | tf_op jit(solution)/shard_map/dot_general | solution.py:22
  33.0 6.8 %fusion.13 = f32[128,4096]{0,1:T(8,128)} fusion(f32[128,4096]{0,1:T(8,128)} %fusion.15, f32[256,4096]{1,0:T(8,128)} %fusion.31, bf16[1,1,4,256,128]{4,3,2,1,0:T(8,128)(2,1)S(1)} %copy-done.4), kind=kOutput, calls=%fused_computation.22 | convolution fusion | flops 544735232 | bytes 10616832 | tf_op jit(solution)/shard_map/dot_general | solution.py:22
  39.8 6.8 %fusion.11 = f32[128,4096]{0,1:T(8,128)} fusion(f32[128,4096]{0,1:T(8,128)} %fusion.13, f32[256,4096]{1,0:T(8,128)} %fusion.27, bf16[1,128,4096]{1,2,0:T(8,128)(2,1)S(1)} %copy.19, bf16[1,1,4,256,128]{4,3,2,1,0:T(8,128)(2,1)S(1)} %copy-done.4), kind=kOutput, calls=%fused_computation.19 | convolution fusion | flops 545783808 | bytes 11665408 | tf_op jit(solution)/shard_map/dot_general | solution.py:22
  46.7 0.8 copy-done.7
  47.5 2.0 copy.18
  49.4 1.3 dynamic-slice
  51.3 288.6 %all-reduce.3.cloned.1.call-done = f32[128,4096]{0,1:T(8,128)} async-done(((f32[128,4096]{0,1:T(8,128)}), f32[128,4096]{0,1:T(8,128)}) %all-reduce.3.cloned.1.call-update) | async-done | bytes 2097168
  339.9 2.8 fusion.18
  343.3 19.5 %reduce = f32[4096,4]{1,0:T(8,128)} reduce(f32[4096,1,4]{2,1,0:T(1,128)S(1)} %bitcast.118, f32[]{:T(128)} %broadcast.39), dimensions={1}, to_apply=%bitcast.100.reduce_sub_computation | reduce | bytes 131076
  362.8 3.9 reshape.44
  366.7 9.4 %all-to-all-start = ((f32[16,1,1024]{2,1,0:T(1,128)}), f32[16,1,1024]{2,1,0:T(1,128)S(1)}, u32[]{:S(2)}, u32[]{:S(2)}) async-start(f32[16,1,1024]{2,1,0:T(1,128)} %reshape.44), calls=%async_computation | async-start | bytes 131072 | tf_op jit(solution)/shard_map/all_to_all | solution.py:70
  376.2 11.2 %all-to-all-done = f32[16,1,1024]{2,1,0:T(1,128)S(1)} async-done(((f32[16,1,1024]{2,1,0:T(1,128)}), f32[16,1,1024]{2,1,0:T(1,128)S(1)}, u32[]{:S(2)}, u32[]{:S(2)}) %all-to-all-start) | async-done | bytes 65568 | tf_op jit(solution)/shard_map/all_to_all | solution.py:70
  387.4 0.8 reduce.1
  388.3 4.7 reshape.45
  393.0 2.2 copy.21
  395.2 102.3 %while.14 = (s32[]{:T(128)}, f32[4,256]{1,0:T(4,128)S(1)}, f32[4,256]{1,0:T(4,128)S(1)}, f32[16,4,256]{2,0,1:T(8,128)S(1)}, s32[16]{0:T(128)S(1)}, /*index=5*/s3...) while((s32[]{:T(128)}, f32[4,256]{1,0:T(4,128)S(1)}, ...), condition=%wide.region_2.3_spmd, body=%wide.region_1.2_spmd.sunk | while | flops 7176 | bytes 37089 | solution.py:39
  397.7 0.6 dynamic_slice.26
  400.9 0.7 fusion.68
  404.1 0.6 dynamic_slice.26
  407.3 0.7 fusion.68
  410.5 0.6 dynamic_slice.26
  413.7 0.7 fusion.68
  416.9 0.6 dynamic_slice.26
  420.0 0.7 fusion.68
  426.4 0.7 fusion.68
  432.8 0.7 fusion.68
  439.2 0.7 fusion.68
  442.5 0.6 dynamic_slice.26
  445.6 0.7 fusion.68
  452.0 0.7 fusion.68
  458.4 0.7 fusion.68
  464.8 0.7 fusion.68
  471.2 0.7 fusion.68
  477.6 0.7 fusion.68
  484.0 0.7 fusion.68
  490.4 0.7 fusion.68
  496.8 0.7 fusion.68
  497.8 14.5 %all_to_all.21 = f32[4,16,256]{2,0,1:T(4,128)} all-to-all(f32[4,16,256]{2,0,1:T(4,128)S(1)} %copy.23), channel_id=1, replica_groups=mesh['region'=16,'worker'=32] {'region'}, dimensions={1} | all-to-all | bytes 131072 | tf_op jit(solution)/shard_map/all_to_all | solution.py:80
  512.4 1.2 copy.24
  513.7 56.7 %all-gather.3.cloned.1.call-done = f32[32,4,4096]{2,1,0:T(4,128)} async-done(((f32[1,4,4096]{2,1,0:T(4,128)}), f32[32,4,4096]{2,1,0:T(4,128)}) %all-gather.3.cloned.1.call-update) | async-done | bytes 2097168 | tf_op jit(solution)/shard_map/all_gather | solution.py:82
  570.4 2.9 broadcast_in_dim.17
  (105 shorter events, 27.1 us)
Async XLA Ops:
  7.2 1.2 copy-start
  7.2 332.8 %all-reduce.3.cloned.1.call-start = ((), (), s32[]{:S(2)}) async-start(), calls=%async_computation.3 | async-start | bytes 4194304
  8.4 3.5 copy-start.4
  17.2 2.6 copy-start.1
  46.6 0.8 copy-start.7
  362.8 13.4 %copy-start.9 = (s32[16]{0:T(128)S(1)}, s32[16]{0:T(128)}, u32[]{:S(2)}) copy-start(s32[16]{0:T(128)} %param.17) | copy-start | bytes 196
  366.7 20.7 %all-to-all-start = ((f32[16,1,1024]{2,1,0:T(1,128)}), f32[16,1,1024]{2,1,0:T(1,128)S(1)}, u32[]{:S(2)}, u32[]{:S(2)}) async-start(f32[16,1,1024]{2,1,0:T(1,128)} %reshape.44), calls=%async_computation | async-start | bytes 131072 | tf_op jit(solution)/shard_map/all_to_all | solution.py:70
  376.2 194.2 %all-gather.3.cloned.1.call-start = ((), (), s32[]{:S(2)}) async-start(), calls=%async_computation.2 | async-start | bytes 2162688 | tf_op jit(solution)/shard_map/all_gather | solution.py:82
  388.2 6.9 %copy-start.3 = (f32[4,256]{1,0:T(4,128)S(1)}, f32[4,256]{1,0:T(4,128)}, u32[]{:S(2)}) copy-start(f32[4,256]{1,0:T(4,128)} %param.15) | copy-start | bytes 12292
  388.3 6.9 %copy-start.6 = (f32[4,256]{1,0:T(4,128)S(1)}, f32[4,256]{1,0:T(4,128)}, u32[]{:S(2)}) copy-start(f32[4,256]{1,0:T(4,128)} %param.16) | copy-start | bytes 12292
  388.3 6.9 %copy-start.10 = (s32[16]{0:T(128)S(1)}, s32[16]{0:T(128)}, u32[]{:S(2)}) copy-start(s32[16]{0:T(128)} %param.18) | copy-start | bytes 196
  388.3 109.3 %copy-start.8 = (s32[16]{0:T(128)S(1)}, s32[16]{0:T(128)}, u32[]{:S(2)}) copy-start(s32[16]{0:T(128)} %param.19) | copy-start | bytes 196
  497.5 75.8 %copy-start.2 = (f32[4,256]{1,0:T(4,128)}, f32[4,256]{1,0:T(4,128)S(1)}, u32[]{:S(2)}) copy-start(f32[4,256]{1,0:T(4,128)S(1)} %get-tuple-element.72) | copy-start | bytes 12292
  497.5 75.7 %copy-start.5 = (f32[4,256]{1,0:T(4,128)}, f32[4,256]{1,0:T(4,128)S(1)}, u32[]{:S(2)}) copy-start(f32[4,256]{1,0:T(4,128)S(1)} %get-tuple-element.73) | copy-start | bytes 12292
Sparse Core Ops, SparseCore 0:
  46.8 293.1 all-reduce.2
  512.5 57.7 all-gather.2
where the time goes:
time: 582 us; the launch traced here: 580 us
  waiting for transfers between devices  357 us (61%)
  loops' own time  62.7 us (11%)
  local copies, waits for them, and re-layouts  50.5 us (9%)
  matrix products  37.8 us (6%)
  other arithmetic  33.8 us (6%)
  between operations  14.9 us (3%)
  blocking collectives  14.5 us (2%)
  starting transfers between devices  9.48 us (2%)
    unnamed x3, waiting for transfers between devices  289 us
    another operation x1, loops' own time, merge_arrivals(): lax.scan(advance, (params_now, momentum_now), jnp.arange(arrival_order.sh...  62.7 us
    all_gather x1, waiting for transfers between devices, local(): worker_params = lax.all_gather(pulled_rows, 'worker', axis=0, tiled=True)  56.7 us
    dot_general x4, matrix products, gradient_of(): lax.dot_general(micro_batch, residual, (((0,), (0,)), ((), ())), preferre...  26.1 us
    unnamed x1, other arithmetic  19.5 us
    unnamed x29, local copies, waits for them, and re-layouts  16.3 us
    all_to_all x1, blocking collectives, local(): lax.all_to_all(pulled, 'region', split_axis=1, concat_axis=2, tiled=True)  14.5 us
  transfers between devices with their start and end apart: 3, of which 3 were waited for; matrix products, arithmetic and copies ran while one was open for 1% of the time, Pallas kernels for 0%

commit v1 on v0

v1 whole, which is shorter than its diff:
```python
import jax
import jax.numpy as jnp
from jax import lax
from jax.experimental import pallas as pl
from jax.experimental.pallas import tpu as pltpu
from jax.sharding import PartitionSpec as P

LOCAL_RATE = 0.3
REGION_BETA = 0.9
REGION_RATE = 1.0
GLOBAL_MU = 0.9
GLOBAL_RATE = 0.7

MESH = pl.DeviceIdType.MESH
F32 = jnp.float32
BF16 = jnp.bfloat16

NZ = 4
NX = 4
H = 256

LAG_A, LAG_B, LAG_C, LAG_D, LAG_E, LAG_F, LAG_G, LAG_H = 1, 2, 2, 2, 2, 2, 2, 1
A, B, C, D, E, F, G, HH = range(8)


def dot(a, b):
    return jnp.dot(a, b, preferred_element_type=F32)


def kernel(
    nr,
    stale_ref,
    order_ref,
    slot_ref,
    x_hbm,
    t_hbm,
    w_hbm,
    mom_hbm,
    par_hbm,
    gmom_hbm,
    mom_hout,
    par_hout,
    gmom_hout,
    wp_hout,
    out_mom,
    out_pm,
    out_wp,
    x_v,
    xt_v,
    t_v,
    w_v,
    s_other,
    s_own,
    r_a,
    r_b,
    s_c,
    r_c,
    d_all,
    d_now,
    weights,
    f_all,
    pm_all,
    pm_oth,
    mo_own,
    mo_oth,
    mo_send,
    g_send,
    x_sem,
    t_sem,
    w_sem,
    mo_sem,
    pm_sem,
    send,
    recv,
    misc_send,
    misc_recv,
    mo_ssem,
    mo_rsem,
    out_sem,
):
    nc = nr // 2
    ny = nr // 2
    steps, tokens, _ = x_v.shape
    scale = LOCAL_RATE / tokens
    workers = NZ * NX * 2
    r = lax.axis_index("region")
    w = lax.axis_index("worker")
    z = w // (NX * 2)
    x = (w // 2) % NX
    c = w % 2

    def wid(zz, xx, cc):
        return (zz * NX + xx) * 2 + cc

    partner = {"worker": wid(z, x, 1 - c)}
    x_of = [(x + i) % NX for i in range(NX)]
    z_of = [(z + i) % NZ for i in range(NZ)]
    x_peer = [{"worker": wid(z, x_of[i], c)} for i in range(NX)]
    z_peer = [{"worker": wid(z_of[i], x, c)} for i in range(NZ)]
    hi = r // ny
    y = r % ny
    hi_peer = {"region": (1 - hi) * ny + y}
    y_peer = [{"region": hi * ny + (y + i) % ny} for i in range(ny)]

    barrier = pltpu.get_barrier_semaphore()
    peers = [partner, hi_peer] + x_peer[1:] + z_peer[1:] + y_peer[1:]
    for peer in peers:
        pl.semaphore_signal(barrier, inc=1, device_id=peer, device_id_type=MESH)

    def put(src, dst, s_sem, r_sem, peer):
        pltpu.make_async_remote_copy(
            src_ref=src, dst_ref=dst, send_sem=s_sem, recv_sem=r_sem, device_id=peer, device_id_type=MESH
        ).start()

    def take(ref, sem):
        pltpu.make_async_copy(ref, ref, sem).wait()

    pltpu.make_async_copy(x_hbm.at[0, 0], x_v, x_sem).start()
    for k in range(nc):
        cols = pl.ds(k * 2 * H, 2 * H)
        pltpu.make_async_copy(t_hbm.at[:, cols], t_v.at[k], t_sem.at[k]).start()
        pltpu.make_async_copy(w_hbm.at[0, :, cols], w_v.at[k], w_sem.at[k]).start()
    for k in range(nc):
        mine = pl.ds(pl.multiple_of((2 * k + c) * H, H), H)
        pltpu.make_async_copy(mom_hbm.at[0, :, mine], mo_own.at[k], mo_sem.at[k]).start()
    pltpu.make_async_copy(par_hbm, pm_all.at[0, 0, 0, 0], pm_sem.at[0]).start()
    pltpu.make_async_copy(gmom_hbm, pm_all.at[0, 0, 0, 1], pm_sem.at[1]).start()

    pltpu.make_async_copy(x_hbm.at[0, 0], x_v, x_sem).wait()
    for s in range(steps):
        xt_v[s] = x_v[s].T
    for i in range(nr):
        weights[i] = 1.0 / (1.0 + jnp.full((8, H), stale_ref[i].astype(F32)))

    def tile(k, half):
        cols = pl.ds(pl.multiple_of(half * H, H), H)
        teach = t_v[k, :, cols].T
        start = w_v[k, :, cols].T.astype(F32)
        now = start
        for s in range(steps):
            v = dot(teach, xt_v[s])
            predicted = dot(now.astype(BF16), xt_v[s])
            residual = (predicted - v * jax.nn.sigmoid(v)).astype(BF16)
            now = now - scale * dot(residual, x_v[s])
        return (start - now).T.reshape(NZ, NX, 8, H)

    def compute(k):
        cols = pl.ds(0, 2 * H)
        pltpu.make_async_copy(t_hbm.at[:, cols], t_v.at[k], t_sem.at[k]).wait()
        pltpu.make_async_copy(w_hbm.at[0, :, cols], w_v.at[k], w_sem.at[k]).wait()
        s_other[k] = tile(k, 1 - c)
        s_own[k] = tile(k, c)

    def send_a(k):
        put(s_other.at[k], r_a.at[k], send.at[A, k], recv.at[A, k], partner)

    def opening():
        pl.semaphore_wait(barrier, len(peers))
        put(par_hbm, pm_all.at[0, 0, 1, 0], misc_send.at[0], misc_recv.at[0], hi_peer)
        put(gmom_hbm, pm_all.at[0, 0, 1, 1], misc_send.at[0], misc_recv.at[0], hi_peer)
        for k in range(nc):
            theirs = pl.ds(pl.multiple_of((2 * k + 1 - c) * H, H), H)
            put(mom_hbm.at[0, :, theirs], mo_oth.at[k], mo_ssem.at[0, k], mo_rsem.at[0, k], partner)
        send_a(0)

    def stage_b(k):
        take(r_a.at[k], recv.at[A, k])
        s_own[k] = s_own[k] + r_a[k]
        for i in range(1, NX):
            put(s_own.at[k, :, x_of[i]], r_b.at[k, i - 1], send.at[B, k], recv.at[B, k], x_peer[i])

    def stage_c(k):
        take(r_b.at[k], recv.at[B, k])
        total = s_own[k, :, x]
        for i in range(NX - 1):
            total = total + r_b[k, i]
        s_c[k] = total
        for i in range(1, NZ):
            put(s_c.at[k, z_of[i]], r_c.at[k, i - 1], send.at[C, k], recv.at[C, k], z_peer[i])

    def both(mine, other):
        low = jnp.where(c == 0, mine, other)
        high = jnp.where(c == 0, other, mine)
        return jnp.concatenate([low, high], axis=0)

    def parts(value):
        low, high = value[:4], value[4:]
        return jnp.where(c == 0, low, high), jnp.where(c == 0, high, low)

    def columns(k):
        return pl.ds(pl.multiple_of((2 * k + c) * H, H), H)

    def stage_d(k):
        take(mo_own.at[k], mo_sem.at[k])
        take(mo_oth.at[k], mo_rsem.at[0, k])
        take(r_c.at[k], recv.at[C, k])
        summed = s_c[k, z]
        for i in range(NZ - 1):
            summed = summed + r_c[k, i]
        momentum = REGION_BETA * both(mo_own[k], mo_oth[k]) + summed / workers
        d_all[k, 0, 0] = REGION_RATE * momentum
        put(d_all.at[k, 0, 0], d_all.at[k, 0, 1], send.at[D, k], recv.at[D, k], hi_peer)
        mine, other = parts(momentum)
        out_mom[k, c] = mine
        mo_send[k] = other
        put(mo_send.at[k], out_mom.at[k, c], mo_ssem.at[1, k], mo_rsem.at[1, k], partner)

    def stage_e(k):
        take(d_all.at[k, 0, 1], recv.at[D, k])
        for i in range(1, ny):
            put(d_all.at[k, 0], d_all.at[k, i], send.at[E, k], recv.at[E, k], y_peer[i])

    def spread():
        take(par_hbm, pm_sem.at[0])
        take(gmom_hbm, pm_sem.at[1])
        take(pm_all.at[0, 0, 1], misc_recv.at[0])
        for i in range(1, ny):
            put(pm_all.at[0, 0], pm_all.at[i // 2, i % 2], misc_send.at[1], misc_recv.at[1], y_peer[i])

    def exchange():
        take(d_all.at[0, pl.ds(1, ny - 1)], misc_recv.at[1])
        put(pm_all.at[:, (y + 1 - c) % 2], pm_oth, misc_send.at[2], misc_recv.at[2], partner)

    def stage_f(k):
        take(d_all.at[k, pl.ds(1, ny - 1)], recv.at[E, k])
        for i in range(ny):
            for h in range(2):
                source = ((hi + h) % 2) * ny + (y - i + ny) % ny
                d_now[source] = weights[source] * d_all[k, i, h]
        owner = 2 * k + c
        away = (y - owner % ny + ny) % ny
        side = (owner // ny + hi) % 2
        params = both(pm_all[away // 2, away % 2, side, 0], pm_oth[away // 2, side, 0])
        momentum = both(pm_all[away // 2, away % 2, side, 1], pm_oth[away // 2, side, 1])
        slot = slot_ref[r]
        pulled = params
        for arrival in range(nr):
            update = d_now[order_ref[arrival]]
            momentum = GLOBAL_MU * momentum + update
            params = params - GLOBAL_RATE * (update + GLOBAL_MU * momentum)
            pulled = jnp.where(slot == arrival, params, pulled)
        f_all[k, z] = pulled
        for i in range(1, NZ):
            put(f_all.at[k, z], f_all.at[k, z], send.at[F, k], recv.at[F, k], z_peer[i])

        @pl.when(2 * k + c == r)
        def _():
            for i, value in enumerate((params, momentum)):
                mine, other = parts(value)
                out_pm[i] = mine
                g_send[i] = other
            put(g_send, out_pm, misc_send.at[3], misc_recv.at[3], partner)

    def stage_g(k):
        take(f_all.at[k, pl.ds(0, NZ - 1)], recv.at[F, k])
        out_wp[:, x, :, columns(k)] = f_all[k]
        for i in range(1, NX):
            put(f_all.at[k], out_wp.at[:, x, :, columns(k)], send.at[G, k], recv.at[G, k], x_peer[i])

    def stage_h(k):
        take(r_b.at[k], recv.at[G, k])
        put(out_wp.at[:, :, :, columns(k)], out_wp.at[:, :, :, columns(k)], send.at[HH, k], recv.at[HH, k], partner)

    def stage_end(k):
        take(r_a.at[k], recv.at[HH, k])
        take(mo_oth.at[k], mo_rsem.at[1, k])
        chunk = pl.ds(pl.multiple_of(2 * k * H, 2 * H), 2 * H)
        pltpu.make_async_copy(out_wp.at[:, :, :, chunk], wp_hout.at[:, :, :, chunk], out_sem.at[0, k]).start()
        for i in range(2):
            half = pl.ds(pl.multiple_of((2 * k + i) * H, H), H)
            pltpu.make_async_copy(out_mom.at[k, i], mom_hout.at[0, :, half], out_sem.at[1 + i, k]).start()
        take(r_a.at[k], send.at[A, k])
        take(r_b.at[k], send.at[B, k])
        take(r_c.at[k], send.at[C, k])
        take(d_all.at[k, 0, 1], send.at[D, k])
        take(d_all.at[k, pl.ds(1, ny - 1)], send.at[E, k])
        take(f_all.at[k, pl.ds(0, NZ - 1)], send.at[F, k])
        take(r_b.at[k], send.at[G, k])
        take(r_a.at[k], send.at[HH, k])
        take(mo_oth.at[k], mo_ssem.at[0, k])
        take(mo_oth.at[k], mo_ssem.at[1, k])

    at_b = LAG_A
    at_c = at_b + LAG_B
    at_d = at_c + LAG_C
    at_e = at_d + LAG_D
    at_f = at_e + LAG_E
    at_g = at_f + LAG_F
    at_h = at_g + LAG_G
    at_end = at_h + LAG_H

    def tick(t, _):
        def when(lag, stage):
            @pl.when((t >= lag) & (t < nc + lag))
            def _():
                stage(t - lag)

        when(0, compute)
        pl.when(t == 1)(opening)

        @pl.when((t >= 1) & (t < nc))
        def _():
            send_a(t)

        when(at_end, stage_end)
        when(at_h, stage_h)
        when(at_g, stage_g)
        pl.when(t == 3)(spread)
        pl.when(t == at_f - 1)(exchange)

        @pl.when(t == at_f)
        def _():
            take(pm_oth, misc_recv.at[2])

        when(at_f, stage_f)
        when(at_e, stage_e)
        when(at_d, stage_d)
        when(at_c, stage_c)
        when(at_b, stage_b)
        return 0

    lax.fori_loop(0, nc + at_end, tick, 0)
    take(pm_all.at[0, 0, 1], misc_send.at[0])
    take(d_all.at[0, pl.ds(1, ny - 1)], misc_send.at[1])
    take(pm_oth, misc_send.at[2])

    @pl.when(r % 2 == c)
    def _():
        take(g_send, misc_send.at[3])

    @pl.when(r % 2 != c)
    def _():
        take(g_send, misc_recv.at[3])

    pltpu.make_async_copy(out_pm.at[0], par_hout, pm_sem.at[0]).start()
    pltpu.make_async_copy(out_pm.at[1], gmom_hout, pm_sem.at[1]).start()

    def written(k, _):
        take(out_wp.at[:, :, :, pl.ds(0, 2 * H)], out_sem.at[0, k])
        take(mo_send.at[k], out_sem.at[1, k])
        take(mo_send.at[k], out_sem.at[2, k])
        return 0

    lax.fori_loop(0, nc, written, 0)
    take(out_pm.at[0], pm_sem.at[0])
    take(out_pm.at[1], pm_sem.at[1])


def hand_on(mom, par, gmom, wp, mom_out, par_out, gmom_out, wp_out):
    mom_out[...] = mom[...]
    par_out[...] = par[...]
    gmom_out[...] = gmom[...]
    wp_out[...] = wp[...]


def local(nr, worker_start, inputs, teacher, regional_momentum, global_params, global_momentum, staleness, arrival_order, pull_slot):
    _, _, steps, tokens, rows = inputs.shape
    nc = nr // 2
    width = 2 * H
    smem = pl.BlockSpec(memory_space=pltpu.SMEM)
    hbm = pl.BlockSpec(memory_space=pltpu.HBM)
    dma = pltpu.SemaphoreType.DMA
    shapes = (
        jax.ShapeDtypeStruct((1, 4, nc * width), F32),
        jax.ShapeDtypeStruct((4, H), F32),
        jax.ShapeDtypeStruct((4, H), F32),
        jax.ShapeDtypeStruct((NZ, NX, 8, nc * width), F32),
    )
    results = pl.pallas_call(
        lambda *refs: kernel(nr, *refs),
        out_shape=shapes,
        in_specs=[smem] * 3 + [hbm] * 6,
        out_specs=(hbm,) * 4,
        scratch_shapes=[
            pltpu.VMEM((nc, 2, 4, H), F32),
            pltpu.VMEM((2, 4, H), F32),
            pltpu.VMEM((NZ, NX, 8, nc * width), F32),
            pltpu.VMEM((steps, tokens, rows), BF16),
            pltpu.VMEM((steps, rows, tokens), BF16),
            pltpu.VMEM((nc, rows, width), BF16),
            pltpu.VMEM((nc, rows, width), BF16),
            pltpu.VMEM((nc, NZ, NX, 8, H), F32),
            pltpu.VMEM((nc, NZ, NX, 8, H), F32),
            pltpu.VMEM((nc, NZ, NX, 8, H), F32),
            pltpu.VMEM((nc, NX - 1, NZ, 8, H), F32),
            pltpu.VMEM((nc, NZ, 8, H), F32),
            pltpu.VMEM((nc, NZ - 1, 8, H), F32),
            pltpu.VMEM((nc, nr // 2, 2, 8, H), F32),
            pltpu.VMEM((nr, 8, H), F32),
            pltpu.VMEM((nr, 8, H), F32),
            pltpu.VMEM((nc, NZ, 8, H), F32),
            pltpu.VMEM((nr // 4, 2, 2, 2, 4, H), F32),
            pltpu.VMEM((nr // 4, 2, 2, 4, H), F32),
            pltpu.VMEM((nc, 4, H), F32),
            pltpu.VMEM((nc, 4, H), F32),
            pltpu.VMEM((nc, 4, H), F32),
            pltpu.VMEM((2, 4, H), F32),
            dma,
            dma((nc,)),
            dma((nc,)),
            dma((nc,)),
            dma((2,)),
            dma((8, nc)),
            dma((8, nc)),
            dma((4,)),
            dma((4,)),
            dma((2, nc)),
            dma((2, nc)),
            dma((3, nc)),
        ],
        compiler_params=pltpu.CompilerParams(
            collective_id=0, has_side_effects=True, vmem_limit_bytes=60 * 2**20
        ),
        cost_estimate=pl.CostEstimate(flops=3300000000, bytes_accessed=5000000, transcendentals=4000000),
        name="outer_step",
    )(
        staleness,
        arrival_order,
        pull_slot,
        inputs,
        teacher,
        worker_start,
        regional_momentum,
        global_params,
        global_momentum,
    )
    whole = [pl.BlockSpec(shape.shape, lambda i, n=len(shape.shape): (0,) * n) for shape in shapes[:3]]
    whole.append(pl.BlockSpec((1, NX, 8, nc * width), lambda i: (i, 0, 0, 0)))
    out_mom, out_par, out_gmom, out_wp = pl.pallas_call(
        hand_on,
        grid=(NZ,),
        out_shape=shapes,
        in_specs=whole,
        out_specs=tuple(whole),
        compiler_params=pltpu.CompilerParams(vmem_limit_bytes=60 * 2**20),
        name="hand_on",
    )(*results)
    return out_mom, out_par, out_gmom, out_wp.reshape(1, rows, nc * width)


def solution(mesh):
    nr = mesh.shape["region"]
    placed = (
        P("region", None, None),
        P("region", "worker", None, None, None),
        P(),
        P("region", "worker", None),
        P("worker", "region"),
        P("worker", "region"),
        P(),
        P(),
        P(),
    )
    return jax.shard_map(
        lambda *args: local(nr, *args),
        mesh=mesh,
        in_specs=placed,
        out_specs=(
            P("region", "worker", None),
            P("worker", "region"),
            P("worker", "region"),
            P("region", None, None),
        ),
        check_vma=False,
    )
```

time: 582 us -> 80.1 us (0.14)
  waiting for transfers between devices: 357 us -> 0 us
  Pallas kernels: 0 us -> 79.2 us
  loops' own time: 62.7 us -> 0 us
  local copies, waits for them, and re-layouts: 50.5 us -> 0 us
  matrix products: 37.8 us -> 0 us
  other arithmetic: 33.8 us -> 0 us
  blocking collectives: 14.5 us -> 0 us
  between operations: 14.9 us -> 0.64 us
  starting transfers between devices: 9.48 us -> 0 us
    unnamed x3 -> x0, waiting for transfers between devices: 289 us -> none
    pallas_call x0 -> x2, Pallas kernels: none -> 79.2 us  [the longest x1 75.4 us: local(): pl.pallas_call(lambda *refs: kernel(nr, *refs), out_shape=shapes, in_spec...]
    another operation x1 -> x0, loops' own time: 62.7 us -> none  [merge_arrivals(): lax.scan(advance, (params_now, momentum_now), jnp.arange(arrival_order.sh...]
    all_gather x1 -> x0, waiting for transfers between devices: 56.7 us -> none  [local(): worker_params = lax.all_gather(pulled_rows, 'worker', axis=0, tiled=True)]
    dot_general x9 -> x0, matrix products: 37.8 us -> none  [the longest x4 26.1 us: gradient_of(): lax.dot_general(micro_batch, residual, (((0,), (0,)), ((), ())), preferre...]
    dynamic_slice x48 -> x0, local copies, waits for them, and re-layouts: 28.2 us -> none  [the longest x16 9.39 us: advance(): source = arrival_order[arrival]]
    unnamed x1 -> x0, other arithmetic: 19.5 us -> none
    unnamed x29 -> x0, local copies, waits for them, and re-layouts: 16.3 us -> none
  transfers between devices with their start and end apart: 3 -> 0, of which waited for: 3 -> 0; matrix products, arithmetic and copies ran while one was open for 1% -> 0% of each run, Pallas kernels for 0% -> 0%
where the time goes in v1:
time: 80.1 us; the launch traced here: 79.8 us
  Pallas kernels  79.2 us (99%)
    pallas_call x1, Pallas kernels, local(): pl.pallas_call(lambda *refs: kernel(nr, *refs), out_shape=shapes, in_spec...  75.4 us
    pallas_call x1, Pallas kernels, local(): pl.pallas_call(hand_on, grid=(NZ,), out_shape=shapes, in_specs=whole, out...  3.8 us

profile of v1, /device:TPU:1, one launch (start us, length us, event | category | flops | bytes accessed | tf_op | source)
XLA Modules:
  0.0 79.8 jit_solution(1913782444800430890)
XLA Ops:
  0.6 75.4 %outer_step.1 = (f32[1,4,4096]{2,1,0:T(4,128)}, f32[4,256]{1,0:T(4,128)}, f32[4,256]{1,0:T(4,128)}, f32[4,4,8,4096]{3,2,1,0:T(8,128)}) custom-call(s32[16]{0:T(128)} %refs_0_.1, s32[16]{0:T(128)} %refs_1_.1, s32[16]{0:T(128)} %refs_2_.1, bf16[1,1,4,256,128]{4,3,2,1,0:T(8,128)(2,1)} %refs_3_.1, bf16[128,4096]{1,0:T(8,128)(2,1)} %refs_4_.1, ...), custom_call_target="tpu_custom_call" | custom-call | flops 3300000000 | bytes 5000000 | tf_op jit(solution)/shard_map/outer_step/pallas_call | solution.py:369
  76.0 3.8 %hand_on.1 = (f32[1,4,4096]{2,1,0:T(4,128)}, f32[4,256]{1,0:T(4,128)}, f32[4,256]{1,0:T(4,128)}, f32[4,4,8,4096]{3,2,1,0:T(8,128)}) custom-call(f32[1,4,4096]{2,1,0:T(4,128)} %get-tuple-element.12.mom, f32[4,256]{1,0:T(4,128)} %get-tuple-element.13.par, f32[4,256]{1,0:T(4,128)} %get-tuple-element.14.gmom, f32[4,4,8,4096]{3,2,1,0:T(8,128)} %get-tuple-element.15.wp), custom_call_target="tpu_custom_call" | custom-call | tf_op jit(solution)/shard_map/hand_on/pallas_call | solution.py:429

commit v2 on v1

--- a/solution.py
+++ b/solution.py
@@ -19,7 +19,8 @@
 NX = 4
 H = 256
 
-LAG_A, LAG_B, LAG_C, LAG_D, LAG_E, LAG_F, LAG_G, LAG_H = 1, 2, 2, 2, 2, 2, 2, 1
+PACE = 2
+LAG_A, LAG_B, LAG_C, LAG_D, LAG_E, LAG_F, LAG_G, LAG_H = 2, 4, 4, 5, 7, 4, 4, 2
 A, B, C, D, E, F, G, HH = range(8)
 
 
@@ -49,8 +50,7 @@
     xt_v,
     t_v,
     w_v,
-    s_other,
-    s_own,
+    s_all,
     r_a,
     r_b,
     s_c,
@@ -132,27 +132,27 @@
     for i in range(nr):
         weights[i] = 1.0 / (1.0 + jnp.full((8, H), stale_ref[i].astype(F32)))
 
-    def tile(k, half):
-        cols = pl.ds(pl.multiple_of(half * H, H), H)
-        teach = t_v[k, :, cols].T
-        start = w_v[k, :, cols].T.astype(F32)
+    def tile(k):
+        teach = t_v[k].T
+        start = w_v[k].T.astype(F32)
         now = start
         for s in range(steps):
             v = dot(teach, xt_v[s])
             predicted = dot(now.astype(BF16), xt_v[s])
             residual = (predicted - v * jax.nn.sigmoid(v)).astype(BF16)
             now = now - scale * dot(residual, x_v[s])
-        return (start - now).T.reshape(NZ, NX, 8, H)
+        return (start - now).T
 
     def compute(k):
         cols = pl.ds(0, 2 * H)
         pltpu.make_async_copy(t_hbm.at[:, cols], t_v.at[k], t_sem.at[k]).wait()
         pltpu.make_async_copy(w_hbm.at[0, :, cols], w_v.at[k], w_sem.at[k]).wait()
-        s_other[k] = tile(k, 1 - c)
-        s_own[k] = tile(k, c)
+        pseudo = tile(k)
+        for half in range(2):
+            s_all[k, half] = pseudo[:, half * H : half * H + H].reshape(NZ, NX, 8, H)
 
     def send_a(k):
-        put(s_other.at[k], r_a.at[k], send.at[A, k], recv.at[A, k], partner)
+        put(s_all.at[k, 1 - c], r_a.at[k], send.at[A, k], recv.at[A, k], partner)
 
     def opening():
         pl.semaphore_wait(barrier, len(peers))
@@ -161,17 +161,16 @@
         for k in range(nc):
             theirs = pl.ds(pl.multiple_of((2 * k + 1 - c) * H, H), H)
             put(mom_hbm.at[0, :, theirs], mo_oth.at[k], mo_ssem.at[0, k], mo_rsem.at[0, k], partner)
-        send_a(0)
 
     def stage_b(k):
         take(r_a.at[k], recv.at[A, k])
-        s_own[k] = s_own[k] + r_a[k]
+        s_all[k, c] = s_all[k, c] + r_a[k]
         for i in range(1, NX):
-            put(s_own.at[k, :, x_of[i]], r_b.at[k, i - 1], send.at[B, k], recv.at[B, k], x_peer[i])
+            put(s_all.at[k, c, :, x_of[i]], r_b.at[k, i - 1], send.at[B, k], recv.at[B, k], x_peer[i])
 
     def stage_c(k):
         take(r_b.at[k], recv.at[B, k])
-        total = s_own[k, :, x]
+        total = s_all[k, c, :, x]
         for i in range(NX - 1):
             total = total + r_b[k, i]
         s_c[k] = total
@@ -291,22 +290,18 @@
 
     def tick(t, _):
         def when(lag, stage):
-            @pl.when((t >= lag) & (t < nc + lag))
+            @pl.when((t >= lag) & (t < PACE * nc + lag) & ((t - lag) % PACE == 0))
             def _():
-                stage(t - lag)
+                stage((t - lag) // PACE)
 
         when(0, compute)
-        pl.when(t == 1)(opening)
-
-        @pl.when((t >= 1) & (t < nc))
-        def _():
-            send_a(t)
-
+        pl.when(t == 0)(opening)
+        when(0, send_a)
         when(at_end, stage_end)
         when(at_h, stage_h)
         when(at_g, stage_g)
-        pl.when(t == 3)(spread)
-        pl.when(t == at_f - 1)(exchange)
+        pl.when(t == 8)(spread)
+        pl.when(t == at_f - 3)(exchange)
 
         @pl.when(t == at_f)
         def _():
@@ -319,7 +314,7 @@
         when(at_b, stage_b)
         return 0
 
-    lax.fori_loop(0, nc + at_end, tick, 0)
+    lax.fori_loop(0, PACE * (nc - 1) + at_end + 1, tick, 0)
     take(pm_all.at[0, 0, 1], misc_send.at[0])
     take(d_all.at[0, pl.ds(1, ny - 1)], misc_send.at[1])
     take(pm_oth, misc_send.at[2])
@@ -346,11 +341,19 @@
     take(out_pm.at[1], pm_sem.at[1])
 
 
-def hand_on(mom, par, gmom, wp, mom_out, par_out, gmom_out, wp_out):
-    mom_out[...] = mom[...]
-    par_out[...] = par[...]
-    gmom_out[...] = gmom[...]
-    wp_out[...] = wp[...]
+def hand_on(*refs):
+    given, made, held, arrive, leave = refs[:4], refs[4:8], refs[8:12], refs[12], refs[13]
+    routes = [(given[3].at[i], held[3].at[i], made[3].at[i]) for i in range(NZ)]
+    routes += [(given[i], held[i], made[i]) for i in range(3)]
+    inward = [pltpu.make_async_copy(src, mid, arrive.at[i]) for i, (src, mid, _) in enumerate(routes)]
+    outward = [pltpu.make_async_copy(mid, dst, leave.at[i]) for i, (_, mid, dst) in enumerate(routes)]
+    for copy in inward:
+        copy.start()
+    for copy, onward in zip(inward, outward):
+        copy.wait()
+        onward.start()
+    for copy in outward:
+        copy.wait()
 
 
 def local(nr, worker_start, inputs, teacher, regional_momentum, global_params, global_momentum, staleness, arrival_order, pull_slot):
@@ -379,8 +382,7 @@
             pltpu.VMEM((steps, rows, tokens), BF16),
             pltpu.VMEM((nc, rows, width), BF16),
             pltpu.VMEM((nc, rows, width), BF16),
-            pltpu.VMEM((nc, NZ, NX, 8, H), F32),
-            pltpu.VMEM((nc, NZ, NX, 8, H), F32),
+            pltpu.VMEM((nc, 2, NZ, NX, 8, H), F32),
             pltpu.VMEM((nc, NZ, NX, 8, H), F32),
             pltpu.VMEM((nc, NX - 1, NZ, 8, H), F32),
             pltpu.VMEM((nc, NZ, 8, H), F32),
@@ -424,14 +426,12 @@
         global_params,
         global_momentum,
     )
-    whole = [pl.BlockSpec(shape.shape, lambda i, n=len(shape.shape): (0,) * n) for shape in shapes[:3]]
-    whole.append(pl.BlockSpec((1, NX, 8, nc * width), lambda i: (i, 0, 0, 0)))
     out_mom, out_par, out_gmom, out_wp = pl.pallas_call(
         hand_on,
-        grid=(NZ,),
         out_shape=shapes,
-        in_specs=whole,
-        out_specs=tuple(whole),
+        in_specs=[hbm] * 4,
+        out_specs=(hbm,) * 4,
+        scratch_shapes=[pltpu.VMEM(shape.shape, F32) for shape in shapes] + [dma((NZ + 3,)), dma((NZ + 3,))],
         compiler_params=pltpu.CompilerParams(vmem_limit_bytes=60 * 2**20),
         name="hand_on",
     )(*results)

time: 80.1 us -> 72.8 us (0.909)
  Pallas kernels: 79.2 us -> 71.9 us
    pallas_call x1, Pallas kernels: 75.4 us -> 69.4 us  [local(): pl.pallas_call(lambda *refs: kernel(nr, *refs), out_shape=shapes, in_spec...]
    pallas_call x1, Pallas kernels: 3.8 us -> 2.49 us  [local(): pl.pallas_call(hand_on, out_shape=shapes, in_specs=[hbm] * 4, out_specs=(...]
where the time goes in v2:
time: 72.8 us; the launch traced here: 72.6 us
  Pallas kernels  71.9 us (99%)
    pallas_call x1, Pallas kernels, local(): pl.pallas_call(lambda *refs: kernel(nr, *refs), out_shape=shapes, in_spec...  69.4 us
    pallas_call x1, Pallas kernels, local(): pl.pallas_call(hand_on, out_shape=shapes, in_specs=[hbm] * 4, out_specs=(...  2.49 us

profile of v2, /device:TPU:1, one launch (start us, length us, event | category | flops | bytes accessed | tf_op | source)
XLA Modules:
  0.0 72.6 jit_solution(2882221069785647203)
XLA Ops:
  0.6 69.4 %outer_step.1 = (f32[1,4,4096]{2,1,0:T(4,128)}, f32[4,256]{1,0:T(4,128)}, f32[4,256]{1,0:T(4,128)}, f32[4,4,8,4096]{3,2,1,0:T(8,128)}) custom-call(s32[16]{0:T(128)} %refs_0_.1, s32[16]{0:T(128)} %refs_1_.1, s32[16]{0:T(128)} %refs_2_.1, bf16[1,1,4,256,128]{4,3,2,1,0:T(8,128)(2,1)} %refs_3_.1, bf16[128,4096]{1,0:T(8,128)(2,1)} %refs_4_.1, ...), custom_call_target="tpu_custom_call" | custom-call | flops 3300000000 | bytes 5000000 | tf_op jit(solution)/shard_map/outer_step/pallas_call | solution.py:372
  70.1 2.5 %hand_on.1 = (f32[1,4,4096]{2,1,0:T(4,128)}, f32[4,256]{1,0:T(4,128)}, f32[4,256]{1,0:T(4,128)}, f32[4,4,8,4096]{3,2,1,0:T(8,128)}) custom-call(f32[1,4,4096]{2,1,0:T(4,128)} %get-tuple-element.12.refs_0_, f32[4,256]{1,0:T(4,128)} %get-tuple-element.13.refs_1_, f32[4,256]{1,0:T(4,128)} %get-tuple-element.14.refs_2_, f32[4,4,8,4096]{3,2,1,0:T(8,128)} %get-tuple-element.15.refs_3_), custom_call_target="tpu_custom_call" | custom-call | tf_op jit(solution)/shard_map/hand_on/pallas_call | solution.py:429

commit v3 on v2

--- a/solution.py
+++ b/solution.py
@@ -165,7 +165,7 @@
     def stage_b(k):
         take(r_a.at[k], recv.at[A, k])
         s_all[k, c] = s_all[k, c] + r_a[k]
-        for i in range(1, NX):
+        for i in (2, 1, 3):
             put(s_all.at[k, c, :, x_of[i]], r_b.at[k, i - 1], send.at[B, k], recv.at[B, k], x_peer[i])
 
     def stage_c(k):
@@ -174,7 +174,7 @@
         for i in range(NX - 1):
             total = total + r_b[k, i]
         s_c[k] = total
-        for i in range(1, NZ):
+        for i in (2, 3, 1):
             put(s_c.at[k, z_of[i]], r_c.at[k, i - 1], send.at[C, k], recv.at[C, k], z_peer[i])
 
     def both(mine, other):
@@ -206,7 +206,7 @@
 
     def stage_e(k):
         take(d_all.at[k, 0, 1], recv.at[D, k])
-        for i in range(1, ny):
+        for i in (4, 3, 5, 2, 6, 1, 7):
             put(d_all.at[k, 0], d_all.at[k, i], send.at[E, k], recv.at[E, k], y_peer[i])
 
     def spread():
@@ -239,7 +239,7 @@
             params = params - GLOBAL_RATE * (update + GLOBAL_MU * momentum)
             pulled = jnp.where(slot == arrival, params, pulled)
         f_all[k, z] = pulled
-        for i in range(1, NZ):
+        for i in (2, 3, 1):
             put(f_all.at[k, z], f_all.at[k, z], send.at[F, k], recv.at[F, k], z_peer[i])
 
         @pl.when(2 * k + c == r)
@@ -253,7 +253,7 @@
     def stage_g(k):
         take(f_all.at[k, pl.ds(0, NZ - 1)], recv.at[F, k])
         out_wp[:, x, :, columns(k)] = f_all[k]
-        for i in range(1, NX):
+        for i in (2, 1, 3):
             put(f_all.at[k], out_wp.at[:, x, :, columns(k)], send.at[G, k], recv.at[G, k], x_peer[i])
 
     def stage_h(k):

time: 72.8 us -> 70.8 us (0.973)
  Pallas kernels: 71.9 us -> 70 us
    pallas_call x1, Pallas kernels: 69.4 us -> 67.5 us  [local(): pl.pallas_call(lambda *refs: kernel(nr, *refs), out_shape=shapes, in_spec...]
where the time goes in v3:
time: 70.8 us; the launch traced here: 70.6 us
  Pallas kernels  70 us (99%)
    pallas_call x1, Pallas kernels, local(): pl.pallas_call(lambda *refs: kernel(nr, *refs), out_shape=shapes, in_spec...  67.5 us
    pallas_call x1, Pallas kernels, local(): pl.pallas_call(hand_on, out_shape=shapes, in_specs=[hbm] * 4, out_specs=(...  2.49 us

profile of v3, /device:TPU:1, one launch (start us, length us, event | category | flops | bytes accessed | tf_op | source)
XLA Modules:
  0.0 70.6 jit_solution(16224845433588162924)
XLA Ops:
  0.6 67.5 %outer_step.1 = (f32[1,4,4096]{2,1,0:T(4,128)}, f32[4,256]{1,0:T(4,128)}, f32[4,256]{1,0:T(4,128)}, f32[4,4,8,4096]{3,2,1,0:T(8,128)}) custom-call(s32[16]{0:T(128)} %refs_0_.1, s32[16]{0:T(128)} %refs_1_.1, s32[16]{0:T(128)} %refs_2_.1, bf16[1,1,4,256,128]{4,3,2,1,0:T(8,128)(2,1)} %refs_3_.1, bf16[128,4096]{1,0:T(8,128)(2,1)} %refs_4_.1, ...), custom_call_target="tpu_custom_call" | custom-call | flops 3300000000 | bytes 5000000 | tf_op jit(solution)/shard_map/outer_step/pallas_call | solution.py:372
  68.1 2.5 %hand_on.1 = (f32[1,4,4096]{2,1,0:T(4,128)}, f32[4,256]{1,0:T(4,128)}, f32[4,256]{1,0:T(4,128)}, f32[4,4,8,4096]{3,2,1,0:T(8,128)}) custom-call(f32[1,4,4096]{2,1,0:T(4,128)} %get-tuple-element.12.refs_0_, f32[4,256]{1,0:T(4,128)} %get-tuple-element.13.refs_1_, f32[4,256]{1,0:T(4,128)} %get-tuple-element.14.refs_2_, f32[4,4,8,4096]{3,2,1,0:T(8,128)} %get-tuple-element.15.refs_3_), custom_call_target="tpu_custom_call" | custom-call | tf_op jit(solution)/shard_map/hand_on/pallas_call | solution.py:429

commit v4 on v3

--- a/solution.py
+++ b/solution.py
@@ -104,9 +104,6 @@
 
     barrier = pltpu.get_barrier_semaphore()
     peers = [partner, hi_peer] + x_peer[1:] + z_peer[1:] + y_peer[1:]
-    for peer in peers:
-        pl.semaphore_signal(barrier, inc=1, device_id=peer, device_id_type=MESH)
-
     def put(src, dst, s_sem, r_sem, peer):
         pltpu.make_async_remote_copy(
             src_ref=src, dst_ref=dst, send_sem=s_sem, recv_sem=r_sem, device_id=peer, device_id_type=MESH
@@ -120,6 +117,9 @@
         cols = pl.ds(k * 2 * H, 2 * H)
         pltpu.make_async_copy(t_hbm.at[:, cols], t_v.at[k], t_sem.at[k]).start()
         pltpu.make_async_copy(w_hbm.at[0, :, cols], w_v.at[k], w_sem.at[k]).start()
+    for peer in peers:
+        pl.semaphore_signal(barrier, inc=1, device_id=peer, device_id_type=MESH)
+
     for k in range(nc):
         mine = pl.ds(pl.multiple_of((2 * k + c) * H, H), H)
         pltpu.make_async_copy(mom_hbm.at[0, :, mine], mo_own.at[k], mo_sem.at[k]).start()
@@ -260,11 +260,13 @@
         take(r_b.at[k], recv.at[G, k])
         put(out_wp.at[:, :, :, columns(k)], out_wp.at[:, :, :, columns(k)], send.at[HH, k], recv.at[HH, k], partner)
 
+        pltpu.make_async_copy(out_wp.at[:, :, :, columns(k)], wp_hout.at[:, :, :, columns(k)], out_sem.at[3, k]).start()
+
     def stage_end(k):
         take(r_a.at[k], recv.at[HH, k])
         take(mo_oth.at[k], mo_rsem.at[1, k])
-        chunk = pl.ds(pl.multiple_of(2 * k * H, 2 * H), 2 * H)
-        pltpu.make_async_copy(out_wp.at[:, :, :, chunk], wp_hout.at[:, :, :, chunk], out_sem.at[0, k]).start()
+        theirs = pl.ds(pl.multiple_of((2 * k + 1 - c) * H, H), H)
+        pltpu.make_async_copy(out_wp.at[:, :, :, theirs], wp_hout.at[:, :, :, theirs], out_sem.at[0, k]).start()
         for i in range(2):
             half = pl.ds(pl.multiple_of((2 * k + i) * H, H), H)
             pltpu.make_async_copy(out_mom.at[k, i], mom_hout.at[0, :, half], out_sem.at[1 + i, k]).start()
@@ -331,7 +333,8 @@
     pltpu.make_async_copy(out_pm.at[1], gmom_hout, pm_sem.at[1]).start()
 
     def written(k, _):
-        take(out_wp.at[:, :, :, pl.ds(0, 2 * H)], out_sem.at[0, k])
+        take(r_a.at[k], out_sem.at[0, k])
+        take(r_a.at[k], out_sem.at[3, k])
         take(mo_send.at[k], out_sem.at[1, k])
         take(mo_send.at[k], out_sem.at[2, k])
         return 0
@@ -408,7 +411,7 @@
             dma((4,)),
             dma((2, nc)),
             dma((2, nc)),
-            dma((3, nc)),
+            dma((4, nc)),
         ],
         compiler_params=pltpu.CompilerParams(
             collective_id=0, has_side_effects=True, vmem_limit_bytes=60 * 2**20

time: 70.8 us -> 70.8 us (level)
  no operation moved by 1% of the time
where the time goes in v4:
time: 70.8 us; the launch traced here: 70.6 us
  Pallas kernels  69.9 us (99%)
    pallas_call x1, Pallas kernels, local(): pl.pallas_call(lambda *refs: kernel(nr, *refs), out_shape=shapes, in_spec...  67.4 us
    pallas_call x1, Pallas kernels, local(): pl.pallas_call(hand_on, out_shape=shapes, in_specs=[hbm] * 4, out_specs=(...  2.49 us

profile of v4, /device:TPU:1, one launch (start us, length us, event | category | flops | bytes accessed | tf_op | source)
XLA Modules:
  0.0 70.6 jit_solution(15502416403908537613)
XLA Ops:
  0.6 67.4 %outer_step.1 = (f32[1,4,4096]{2,1,0:T(4,128)}, f32[4,256]{1,0:T(4,128)}, f32[4,256]{1,0:T(4,128)}, f32[4,4,8,4096]{3,2,1,0:T(8,128)}) custom-call(s32[16]{0:T(128)} %refs_0_.1, s32[16]{0:T(128)} %refs_1_.1, s32[16]{0:T(128)} %refs_2_.1, bf16[1,1,4,256,128]{4,3,2,1,0:T(8,128)(2,1)} %refs_3_.1, bf16[128,4096]{1,0:T(8,128)(2,1)} %refs_4_.1, ...), custom_call_target="tpu_custom_call" | custom-call | flops 3300000000 | bytes 5000000 | tf_op jit(solution)/shard_map/outer_step/pallas_call | solution.py:375
  68.1 2.5 %hand_on.1 = (f32[1,4,4096]{2,1,0:T(4,128)}, f32[4,256]{1,0:T(4,128)}, f32[4,256]{1,0:T(4,128)}, f32[4,4,8,4096]{3,2,1,0:T(8,128)}) custom-call(f32[1,4,4096]{2,1,0:T(4,128)} %get-tuple-element.12.refs_0_, f32[4,256]{1,0:T(4,128)} %get-tuple-element.13.refs_1_, f32[4,256]{1,0:T(4,128)} %get-tuple-element.14.refs_2_, f32[4,4,8,4096]{3,2,1,0:T(8,128)} %get-tuple-element.15.refs_3_), custom_call_target="tpu_custom_call" | custom-call | tf_op jit(solution)/shard_map/hand_on/pallas_call | solution.py:432
